TPU v7x, 512 devices: a whole 4x8x8 slice. The times are simulated.
512 devices in a mesh: gossip: 16 (over y, x_lo), fsdp: 32 (over x_hi, z, core).
Axes of the slice: x: 4 (x_hi: 2, x_lo: 2; x = x_hi * 2 + x_lo), y: 8, z: 8, core: 2. Of those that a mesh axis runs over, the one named last changes fastest.
Arguments:
- block_input: bfloat16 [16, 6144, 1024], P('gossip', 'fsdp'), may hold values from -6 to 6
- preact: bfloat16 [16, 6144, 2048], P('gossip', 'fsdp'), may hold values from -6 to 6
- cotangent: bfloat16 [16, 6144, 1024], P('gossip', 'fsdp'), may hold values from -6 to 6
- seq_ids: int32 [16, 6144], P('gossip', 'fsdp'), may hold values from 0 to 7, never falling along the last dimension, each value on 1 to 1536 neighbouring positions
- gates: float32 [16, 8, 1024], P('gossip'), may hold values from -5 to 5
- weight: float32 [16, 2048, 1024], P('gossip', 'fsdp'), may hold values from -6 to 6
- first_moment: float32 [16, 2048, 1024], P('gossip', 'fsdp'), may hold values from -4 to 4
- second_moment: float32 [16, 2048, 1024], P('gossip', 'fsdp'), may hold values from 0.1 to 4
- step: int32 [], replicated, may hold values from 0 to 63
Outputs:
- block_output: bfloat16 [16, 6144, 1024], P('gossip', 'fsdp')
- preact_grad: bfloat16 [16, 6144, 2048], P('gossip', 'fsdp')
- gate_grad: float32 [16, 8, 1024], P('gossip')
- weight_out: float32 [16, 2048, 1024], P('gossip', 'fsdp')
- first_out: float32 [16, 2048, 1024], P('gossip', 'fsdp')
- second_out: float32 [16, 2048, 1024], P('gossip', 'fsdp')
Inputs may be any that keep to these rules, and one draw needn't show every extreme that they name: `seq_ids`: sequences are runs of consecutive tokens of 1 to 1536, numbered in order; one run has exactly 1536 tokens.
All inputs are finite; a program needn't handle non-finite values.
Results may differ from a plain program's by a relative error of at most 0.017.
Values may be sent and summed in bfloat16 or wider, within the bound.
A program may use at most 64 MiB of HBM per device.

v0:
```python
from functools import partial

import jax
import jax.numpy as jnp
from jax import lax
from jax.sharding import PartitionSpec as P


def shortened(array):

    def short(part):
        return part.astype(jnp.bfloat16) if part.dtype == jnp.float32 else part

    return jax.tree.map(short, array)


def shifted(value, axis, steps):
    count = lax.axis_size(axis)
    pairs = [(source, (source + steps) % count) for source in range(count)]
    return lax.ppermute(value, axis, pairs)


def gelu_parts(values):
    inner = 0.7978845608 * (values + 0.044715 * values * values * values)
    tangent = jnp.tanh(inner)
    activated = 0.5 * values * (1.0 + tangent)
    slope = 0.5 * (1.0 + tangent) + 0.5 * values * (1.0 - tangent * tangent) * 0.7978845608 * (
        1.0 + 3.0 * 0.044715 * values * values
    )
    return (activated, slope)


def peer_rows(values, distance):
    return jax.tree.map(
        lambda part, own: part.astype(own.dtype),
        shifted(shortened(values), "gossip", distance),
        values,
    )


def on_device(
    block_input, preact, cotangent, seq_ids, gates, weight, first_moment, second_moment, step
):
    pre_vals = preact[0].astype(jnp.float32)
    activated, slope = gelu_parts(pre_vals)
    hidden = activated.astype(jnp.bfloat16)
    scaling = hidden.shape[1] ** (-0.5)
    weight_low = weight[0].astype(jnp.bfloat16)
    columns = hidden
    projected = (
        jnp.dot(
            columns,
            lax.all_gather(weight_low, "fsdp", axis=0, tiled=True),
            preferred_element_type=jnp.float32,
        )
        * scaling
    )
    seq_count = gates.shape[1]
    one_hot = (seq_ids[0][:, None] == jnp.arange(seq_count, dtype=jnp.int32)[None, :]).astype(
        jnp.float32
    )
    token_gate = jnp.dot(one_hot, gates[0], precision=lax.Precision.HIGHEST)
    block_output = (block_input[0].astype(jnp.float32) + token_gate * projected).astype(
        jnp.bfloat16
    )
    cot_vals = cotangent[0].astype(jnp.float32)
    scaled_cot = (token_gate * cot_vals).astype(jnp.bfloat16)
    gate_local = jnp.dot(one_hot.T, cot_vals * projected, precision=lax.Precision.HIGHEST)
    gate_grad = lax.psum(gate_local.astype(jnp.bfloat16), "fsdp").astype(jnp.float32)
    columns = hidden
    product = lax.dot_general(
        columns, scaled_cot, (((0,), (0,)), ((), ())), preferred_element_type=jnp.float32
    )
    grad = lax.psum_scatter(
        (product * scaling).astype(jnp.bfloat16), "fsdp", scatter_dimension=0, tiled=True
    ).astype(jnp.float32)
    hidden_grad = (
        lax.dot_general(
            scaled_cot,
            lax.all_gather(weight_low, "fsdp", axis=0, tiled=True),
            (((1,), (1,)), ((), ())),
            preferred_element_type=jnp.float32,
        )
        * scaling
    )
    preact_grad = (hidden_grad * slope).astype(jnp.bfloat16)
    counter = (step + 1).astype(jnp.float32)
    corr_first = 1.0 - jnp.power(jnp.float32(0.9), counter)
    corr_second = 1.0 - jnp.power(jnp.float32(0.999), counter)
    master = weight[0]
    first_new = 0.9 * first_moment[0] + 0.1 * grad
    second_new = 0.999 * second_moment[0] + 0.001 * grad * grad
    update = first_new / corr_first / (jnp.sqrt(second_new / corr_second) + 1e-08)
    stepped = master - 0.01 * (update + 0.1 * master)
    levels = lax.axis_size("gossip").bit_length() - 1
    branches = [partial(peer_rows, distance=1 << level) for level in range(levels)]
    received = lax.switch(step % levels, branches, stepped)
    weight_out = 0.5 * (stepped + received)
    return (
        block_output[None],
        preact_grad[None],
        gate_grad[None],
        weight_out[None],
        first_new[None],
        second_new[None],
    )


def solution(mesh):
    return jax.shard_map(
        on_device,
        mesh=mesh,
        in_specs=(
            P("gossip", "fsdp", None),
            P("gossip", "fsdp", None),
            P("gossip", "fsdp", None),
            P("gossip", "fsdp"),
            P("gossip", None, None),
            P("gossip", "fsdp", None),
            P("gossip", "fsdp", None),
            P("gossip", "fsdp", None),
            P(),
        ),
        out_specs=(
            P("gossip", "fsdp", None),
            P("gossip", "fsdp", None),
            P("gossip", None, None),
            P("gossip", "fsdp", None),
            P("gossip", "fsdp", None),
            P("gossip", "fsdp", None),
        ),
        check_vma=False,
    )
```

profile of v0, /device:TPU:1, one launch (start us, length us, event | category | flops | bytes accessed | tf_op | source)
XLA Modules:
  0.0 393.5 jit_solution(9187155396152728894)
XLA Ops:
  7.2 0.0 copy-start
  7.2 0.0 reduce-scatter.2.cloned.1.call-start
  7.2 0.7 copy-done
  7.9 1.2 fusion.23
  9.1 5.0 %multiply_convert_fusion = bf16[2048,1024]{1,0:T(8,128)(2,1)} fusion(f32[192,1024]{1,0:T(8,128)S(1)} %fusion.23, bf16[1,192,1024]{2,1,0:T(8,128)(2,1)} %param.15, bf16[1,192,2048]{2,1,0:T(8,128)(2,1)} %param.14), kind=kOutput, calls=%fused_computation | convolution fusion | flops 814022656 | bytes 6160384 | tf_op jit(solution)/shard_map/dot_general | solution.py:71
  14.1 0.0 copy-start.1
  14.1 0.0 copy-start.4
  14.1 0.0 reduce-scatter.2.cloned.1.call-update
  14.1 0.0 all-gather.2.cloned.1.call-start
  14.2 0.9 copy-done.1
  15.0 0.7 bitcast_convert_fusion
  15.7 0.0 all-gather.2.cloned.1.call-update
  16.5 135.3 %reduce-scatter.2.cloned.1.call-done = bf16[64,1024]{1,0:T(8,128)(2,1)} async-done(((bf16[2048,1024]{1,0:T(8,128)(2,1)}), bf16[64,1024]{1,0:T(8,128)(2,1)}) %reduce-scatter.2.cloned.1.call-update) | async-done | bytes 131088 | tf_op jit(solution)/shard_map/reduce_scatter | solution.py:74
  151.7 0.0 copy-done.4
  151.7 0.0 copy-done.5
  151.7 1.9 fusion.22
  153.6 0.0 copy-start.7
  153.6 7.1 %conditional.4 = (f32[64,1024]{1,0:T(8,128)S(1)}) conditional(s32[]{:T(128)} %clamp.3, f32[64,1024]{1,0:T(8,128)S(1)} %get-tuple-element.22, f32[64,1024]{1,0:T(8,128)S(1)} %get-tuple-element.22, f32[64,1024]{1,0:T(8,128)S(1)} %get-tuple-element.22, f32[64,1024]{1,0:T(8,128)S(1)} %get-tuple-element.22), branch_computations={%region_2.3_spmd, %region_3.4_spmd, %region_4.5_spmd, %region_5.6_... | conditional | flops 131072 | bytes 1310768
  153.7 3.2 collective-permute-start.1
  156.9 3.8 collective-permute-done.1
  160.7 0.7 multiply_bitcast_fusion
  161.5 90.2 %all-gather.2.cloned.1.call-done = bf16[2048,1024]{1,0:T(8,128)(2,1)} async-done(((bf16[64,1024]{1,0:T(8,128)(2,1)}), bf16[2048,1024]{1,0:T(8,128)(2,1)}) %all-gather.2.cloned.1.call-update) | async-done | bytes 4194320 | tf_op jit(solution)/shard_map/all_gather | solution.py:53
  251.7 0.0 copy-done.7
  251.7 3.4 convolution_multiply_fusion.1
  255.1 0.0 copy-done.3
  255.1 0.0 copy-done.6
  255.1 0.5 fusion.12
  255.6 0.0 copy-done.2
  255.6 0.9 fusion.15
  256.5 124.2 %psum.7 = bf16[1,8,1024]{2,1,0:T(8,128)(2,1)S(1)} all-reduce(bf16[1,8,1024]{2,1,0:T(8,128)(2,1)S(1)} %fusion.12), channel_id=1, replica_groups=mesh['gossip'=16,'fsdp'=32] {'fsdp'}, use_global_device_ids=true, to_apply=%region_0.0 | all-reduce | flops 8192 | bytes 32768 | tf_op jit(solution)/shard_map/psum | solution.py:69
  380.8 0.6 broadcast_in_dim.25
  381.4 5.3 %fusion.2 = bf16[1,192,2048]{2,1,0:T(8,128)(2,1)} fusion(bf16[2048,1024]{1,0:T(8,128)(2,1)} %all-gather.2.cloned.1.call-done, bf16[1,192,2048]{2,1,0:T(8,128)(2,1)S(1)} %copy-done.7, f32[192,1024]{1,0:T(8,128)S(1)} %fusion.23, bf16[1,192,1024]{2,1,0:T(8,128)(2,1)S(1)} %copy-done.3), kind=kOutput, calls=%fused_computation.11 | convolution fusion | flops 814153728 | bytes 6946816 | tf_op jit(solution)/shard_map/dot_general | solution.py:78
  (6 shorter events, 0.0 us)
Async XLA Ops:
  7.2 0.8 copy-start
  7.2 144.6 %reduce-scatter.2.cloned.1.call-start = ((), (), s32[]{:S(2)}) async-start(), calls=%async_computation.2 | async-start | bytes 4325376 | tf_op jit(solution)/shard_map/reduce_scatter | solution.py:74
  14.1 0.9 copy-start.1
  14.1 137.7 %copy-start.4 = (f32[1,64,1024]{2,1,0:T(8,128)S(1)}, f32[1,64,1024]{2,1,0:T(8,128)}, u32[]{:S(2)}) copy-start(f32[1,64,1024]{2,1,0:T(8,128)} %param.20) | copy-start | bytes 786436
  14.1 137.7 %copy-start.5 = (f32[1,64,1024]{2,1,0:T(8,128)S(1)}, f32[1,64,1024]{2,1,0:T(8,128)}, u32[]{:S(2)}) copy-start(f32[1,64,1024]{2,1,0:T(8,128)} %param.19) | copy-start | bytes 786436
  14.1 237.6 %all-gather.2.cloned.1.call-start = ((), (), s32[]{:S(2)}) async-start(), calls=%async_computation.1 | async-start | bytes 4325376 | tf_op jit(solution)/shard_map/all_gather | solution.py:53
  153.6 98.1 %copy-start.7 = (bf16[1,192,2048]{2,1,0:T(8,128)(2,1)S(1)}, bf16[1,192,2048]{2,1,0:T(8,128)(2,1)}, u32[]{:S(2)}) copy-start(bf16[1,192,2048]{2,1,0:T(8,128)(2,1)} %param.14) | copy-start | bytes 2359300
  153.7 7.1 %collective-permute-start.1 = (bf16[64,1024]{1,0:T(8,128)(2,1)S(1)}, bf16[64,1024]{1,0:T(8,128)(2,1)S(1)}, u32[]{:S(2)}, u32[]{:S(2)}) collective-permute-start(bf16[64,1024]{1,0:T(8,128)(2,1)S(1)} %convert_element_type.60), channel_id=1, source_target_pairs={{0,64},{32,96},{64,128},{96,160},{128,192},{160,224},{192,256},{22... | collective-permute-start | bytes 393224 | tf_op jit(solution)/shard_map/cond/branch_1_fun/ppermute | solution.py:20
  161.5 93.6 %copy-start.3 = (bf16[1,192,1024]{2,1,0:T(8,128)(2,1)S(1)}, bf16[1,192,1024]{2,1,0:T(8,128)(2,1)}, u32[]{:S(2)}) copy-start(bf16[1,192,1024]{2,1,0:T(8,128)(2,1)} %param.15) | copy-start | bytes 1179652
  161.5 93.6 %copy-start.6 = (s32[1,192]{1,0:T(1,128)S(1)}, s32[1,192]{1,0:T(1,128)}, u32[]{:S(2)}) copy-start(s32[1,192]{1,0:T(1,128)} %param.16) | copy-start | bytes 2308
  161.5 94.1 %copy-start.2 = (bf16[1,192,1024]{2,1,0:T(8,128)(2,1)S(1)}, bf16[1,192,1024]{2,1,0:T(8,128)(2,1)}, u32[]{:S(2)}) copy-start(bf16[1,192,1024]{2,1,0:T(8,128)(2,1)} %param.13) | copy-start | bytes 1179652
Sparse Core Ops, SparseCore 0:
  14.2 137.4 reduce-scatter.1
  156.2 95.4 all-gather.1
where the time goes:
time: 398 us; the launch traced here: 393 us
  waiting for transfers between devices  229 us (58%)
  blocking collectives  124 us (31%)
  matrix products  15.2 us (4%)
  between operations  14.8 us (4%)
  other arithmetic  4.89 us (1%)
    reduce_scatter x1, waiting for transfers between devices, on_device(): lax.psum_scatter((product * scaling).astype(jnp.bfloat16), 'fsdp', scatte...  135 us
    psum x1, blocking collectives, on_device(): lax.psum(gate_local.astype(jnp.bfloat16), 'fsdp').astype(jnp.float32)  124 us
    all_gather x1, waiting for transfers between devices, on_device(): lax.all_gather(weight_low, 'fsdp', axis=0, tiled=True)  90.2 us
  transfers between devices with their start and end apart: 3, of which 3 were waited for; matrix products, arithmetic and copies ran while one was open for 1% of the time, Pallas kernels for 0%

commit v1 on v0

v1 whole, which is shorter than its diff:
```python
import functools

import jax
import jax.numpy as jnp
from jax import lax
from jax.experimental import pallas as pl
from jax.experimental.pallas import tpu as pltpu
from jax.sharding import PartitionSpec as P

MESH = pl.DeviceIdType.MESH
BF16, F32 = jnp.bfloat16, jnp.float32

TOK, FFW, D, SEQS = 192, 2048, 1024, 8
ROWS, HALF = 64, 512
NZ = 8
N_GOSSIP = 16

GATHER_HOPS = ((4, 3), (3, 4), (4, 3))
SUM_HOPS = ((3, 4), (4, 3), (3, 4))
X_ORDER = (4, 3, -3, 2, -2, 1, -1, 0)
PEERS = tuple(range(1, NZ))


def kernel(
    shift,
    step_ref, seq_ref, gates_ref, w_h, m1_h, m2_h, pre_h, cot_h, bi_h,
    bo_h, pg_h, gg_h, wo_h, fo_h, so_h,
    w_v, m1_v, m2_v, pre_v, cot_v, bi_v,
    wg, hid, slope_v, ht, hts, sc, scs, tg_v,
    part, rz, rx, rxa,
    gl, gl_r, gx, gx_r, gz, gg_o, gg_r,
    st_v, st_s, st_r, bo_v, pg_v, gg_v, wo_v, fo_v, so_v,
    lsem, osem,
    agz_s, agz_r, agx_s, agx_r, ags_s, ags_r,
    tok_s, tok_r, rsz_s, rsz_r, rsx_s, rsx_r, gg_ss, gg_rs, go_s, go_r,
):
    g = lax.axis_index("gossip")
    f = lax.axis_index("fsdp")
    xh = lax.div(f, 16)
    z = lax.rem(lax.div(f, 2), NZ)
    c = lax.rem(f, 2)
    xo, co = 1 - xh, 1 - c
    scaling = FFW ** -0.5

    def zat(k):
        return lax.rem(z + (k % NZ), NZ)

    def dev(xx, zz, cc):
        return {"fsdp": xx * 16 + zz * 2 + cc}

    znext = (dev(xh, zat(1), c), dev(xh, zat(-1), c))
    xdev, sdev = dev(xo, z, c), dev(xh, z, co)
    up = {"gossip": lax.rem(g + shift, N_GOSSIP)}
    down = {"gossip": lax.rem(g + N_GOSSIP - shift, N_GOSSIP)}

    sent = []

    def describe(src, dst, ssem, rsem, to):
        return pltpu.make_async_remote_copy(
            src_ref=src, dst_ref=dst, send_sem=ssem, recv_sem=rsem, device_id=to, device_id_type=MESH
        )

    def send(src, dst, ssem, rsem, to):
        copy = describe(src, dst, ssem, rsem, to)
        copy.start()
        sent.append(copy)

    def arrive(dst, ssem, rsem, to):
        describe(dst, dst, ssem, rsem, to).wait_recv()

    loads = []
    for i, (src, dst) in enumerate(
        ((w_h, w_v), (cot_h, cot_v), (pre_h, pre_v), (bi_h, bi_v), (m1_h, m1_v), (m2_h, m2_v))
    ):
        copy = pltpu.make_async_copy(src, dst, lsem.at[i])
        copy.start()
        loads.append(copy)
    load_w, load_cot, load_pre, load_bi, load_m1, load_m2 = loads

    barrier = pltpu.get_barrier_semaphore()
    greeted = [xdev, sdev, down] + [dev(xh, zat(k), c) for k in PEERS]
    for to in greeted:
        pl.semaphore_signal(barrier, inc=1, device_id=to, device_id_type=MESH)

    def place(h, xx, zz, cc):
        return wg.at[h, xx * 16 + zz * 2 + cc]

    load_w.wait()
    for h in range(2):
        wg[h, f] = w_v[:, h * HALF:(h + 1) * HALF].astype(BF16)
    pl.semaphore_wait(barrier, len(greeted))

    def gather_x(h, j, zz):
        block = place(h, xh, zz, c)
        i = 9 * h + j
        send(block, block, agx_s.at[i], agx_r.at[i], xdev)

    def gather_x_arrive(h, j, zz):
        i = 9 * h + j
        arrive(place(h, xo, zz, c), agx_s.at[i], agx_r.at[i], xdev)

    def gather_s(h, rel, j, xx, zz):
        block = place(h, xx, zz, c)
        i = 18 * h + 9 * rel + j
        send(block, block, ags_s.at[i], ags_r.at[i], sdev)

    def gather_z(stream, way, s, h, xx, zz):
        block = place(h, xx, zz, c)
        i = 8 * stream + 4 * way + s - 1
        send(block, block, agz_s.at[i], agz_r.at[i], znext[way])

    stream_of = ((0, xh, 0), (0, xo, 1), (1, xh, 0))

    def gather_step(stream, s):
        h, xx, rel = stream_of[stream]
        for way in range(2):
            hops = GATHER_HOPS[stream][way]
            if s > hops:
                continue
            zz = zat(-s if way == 0 else s)
            i = 8 * stream + 4 * way + s - 1
            arrive(place(h, xx, zz, c), agz_s.at[i], agz_r.at[i], znext[way])
            if s < hops:
                gather_z(stream, way, s + 1, h, xx, zz)
            j = 1 + 4 * way + s - 1
            if stream == 2:
                gather_x(1, j, zz)
            gather_s(h, rel, j, xx, zz)

    gather_x(0, 0, z)
    for way in range(2):
        gather_z(0, way, 1, 0, xh, z)
    for way in range(2):
        gather_z(2, way, 1, 1, xh, z)
    gather_x(1, 0, z)
    for h in range(2):
        gather_s(h, 0, 0, xh, z)

    onehot = lax.broadcasted_iota(jnp.int32, (SEQS, TOK), 0) == jnp.broadcast_to(seq_ref[...], (SEQS, TOK))
    onehot = jnp.where(onehot, 1.0, 0.0).astype(F32)
    gates = gates_ref[...]
    hi = gates.astype(BF16).astype(F32)
    mid = (gates - hi).astype(BF16).astype(F32)
    low = (gates - hi - mid).astype(BF16).astype(F32)
    select = jnp.concatenate([onehot] * 3, axis=0).T.astype(BF16)
    tg_v[...] = jnp.dot(
        select, jnp.concatenate([hi, mid, low], axis=0).astype(BF16), preferred_element_type=F32
    )
    load_cot.wait()
    for h in range(2):
        cols = slice(h * HALF, (h + 1) * HALF)
        sc[h] = (tg_v[:, cols] * cot_v[:, cols].astype(F32)).astype(BF16)
    send(sc, scs, tok_s.at[0], tok_r.at[0], sdev)

    gather_x_arrive(0, 0, z)
    for way in range(2):
        gather_z(1, way, 1, 0, xo, z)
    gather_s(0, 1, 0, xo, z)

    load_pre.wait()

    def gelu(xx, j):
        cols = pl.ds(pl.multiple_of((xx * NZ + j) * 128, 128), 128)
        u = pre_v[:, cols].astype(F32)
        sq = u * u
        th = jnp.tanh(0.7978845608 * (u + 0.044715 * sq * u))
        slope_v[:, cols] = 0.5 * (1.0 + th) + 0.5 * u * (1.0 - th * th) * 0.7978845608 * (
            1.0 + 3.0 * 0.044715 * sq
        )
        low_hidden = (0.5 * u * (1.0 + th)).astype(BF16)
        hid[:, cols] = low_hidden
        ht[xx, j] = low_hidden.T.reshape(2, ROWS, TOK)

    def gelu_run(xx):
        @pl.loop(0, NZ)
        def _(j):
            gelu(xx, j)

    gelu_run(xo)
    send(ht.at[xo, :, co], hts.at[xo], tok_s.at[1], tok_r.at[1], sdev)
    gather_step(0, 1)
    gather_step(2, 1)
    gelu_run(xh)
    send(ht.at[xh, :, co], hts.at[xh], tok_s.at[2], tok_r.at[2], sdev)
    gather_step(1, 1)
    gather_step(0, 2)
    gather_step(2, 2)

    def grad(h, xx):
        own = ht[xx, :, c].reshape(NZ * ROWS, TOK)
        other = hts[xx].reshape(NZ * ROWS, TOK)
        total = jnp.dot(own, sc[h], preferred_element_type=F32)
        total += jnp.dot(other, scs[h], preferred_element_type=F32)
        part[h, xx] = (total * scaling).astype(BF16).reshape(NZ, ROWS, HALF)

    slots = rz.at

    def sum_step(stream, s):
        h, xx = ((0, xo), (0, xh), (1, xh))[stream]
        for way in range(2):
            hops = SUM_HOPS[stream][way]
            if s > hops:
                continue
            off = (hops - s + 1) * (1 if way == 0 else -1)
            zz = zat(off)
            block = part.at[h, xx, zz]
            i = 8 * stream + 4 * way + s - 1
            if s > 1 or stream == 2:
                value = block[...].astype(F32)
                if stream == 2:
                    jx = X_ORDER.index(4 if off == -4 else off)
                    arrive(rx.at[jx], rsx_s.at[jx], rsx_r.at[jx], xdev)
                    value += rx[jx].astype(F32)
                if s > 1:
                    arrive(slots[i - 1], rsz_s.at[i - 1], rsz_r.at[i - 1], znext[way])
                    value += rz[i - 1].astype(F32)
                block[...] = value.astype(BF16)
            send(block, slots[i], rsz_s.at[i], rsz_r.at[i], znext[way])

    def sum_last(stream):
        h, xx = ((0, xo), (0, xh), (1, xh))[stream]
        value = part[h, xx, z].astype(F32)
        if stream == 2:
            arrive(rx.at[7], rsx_s.at[7], rsx_r.at[7], xdev)
            value += rx[7].astype(F32)
        for way in range(2):
            i = 8 * stream + 4 * way + SUM_HOPS[stream][way] - 1
            arrive(slots[i], rsz_s.at[i], rsz_r.at[i], znext[way])
            value += rz[i].astype(F32)
        return value

    arrive(scs, tok_s.at[0], tok_r.at[0], sdev)
    arrive(hts.at[xo], tok_s.at[1], tok_r.at[1], sdev)
    grad(1, xo)
    for j, off in enumerate(X_ORDER):
        send(part.at[1, xo, zat(off)], rx.at[j], rsx_s.at[j], rsx_r.at[j], xdev)
    grad(0, xo)
    sum_step(0, 1)
    gather_step(1, 2)
    arrive(hts.at[xh], tok_s.at[2], tok_r.at[2], sdev)
    grad(0, xh)
    sum_step(1, 1)
    gather_step(0, 3)
    gather_step(2, 3)
    grad(1, xh)
    gather_step(1, 3)
    sum_step(0, 2)
    sum_step(1, 2)
    sum_step(2, 1)
    for stream in range(3):
        gather_step(stream, 4)
    sum_step(0, 3)
    sum_step(1, 3)
    sum_step(2, 2)

    def offsets(stream):
        yield 0, 0
        for way in range(2):
            for s in range(1, GATHER_HOPS[stream][way] + 1):
                yield 1 + 4 * way + s - 1, (-s if way == 0 else s)

    def gather_rest(h):
        if h == 1:
            for j, off in offsets(2):
                gather_x_arrive(1, j, zat(off))
                gather_s(1, 1, j, xo, zat(off))
        for rel, xx, stream in ((0, xh, 2 * h), (1, xo, 1 + h)):
            for j, off in offsets(stream):
                i = 18 * h + 9 * rel + j
                arrive(place(h, xx, zat(off), co), ags_s.at[i], ags_r.at[i], sdev)

    outs = []

    def out(src, dst):
        copy = pltpu.make_async_copy(src, dst, osem.at[len(outs)])
        copy.start()
        outs.append(copy)

    def forward(h):
        cols = slice(h * HALF, (h + 1) * HALF)
        projected = jnp.dot(hid[...], wg[h].reshape(FFW, HALF), preferred_element_type=F32) * scaling
        bo_v[:, cols] = (bi_v[:, cols].astype(F32) + tg_v[:, cols] * projected).astype(BF16)
        out(bo_v.at[:, cols], bo_h.at[:, cols])
        product = cot_v[:, cols].astype(F32) * projected
        hi = product.astype(BF16)
        low = (product - hi.astype(F32)).astype(BF16)
        pick = onehot.astype(BF16)
        gl[h] = jnp.dot(pick, hi, preferred_element_type=F32) + jnp.dot(pick, low, preferred_element_type=F32)

    load_bi.wait()
    gather_rest(0)
    forward(0)
    sum_step(0, 4)
    sum_step(1, 4)
    sum_step(2, 3)
    gather_rest(1)
    forward(1)

    send(gl.at[co], gl_r, gg_ss.at[0], gg_rs.at[0], sdev)
    sum_step(2, 4)

    def backward(q):
        rows = wg.at[0, pl.ds(q * 8, 8)][...].reshape(HALF, HALF), wg.at[1, pl.ds(q * 8, 8)][...].reshape(HALF, HALF)
        cols = slice(q * HALF, (q + 1) * HALF)
        dims = (((1,), (1,)), ((), ()))
        total = lax.dot_general(sc[0], rows[0], dims, preferred_element_type=F32)
        total += lax.dot_general(sc[1], rows[1], dims, preferred_element_type=F32)
        pg_v[:, cols] = (total * scaling * slope_v[:, cols]).astype(BF16)
        out(pg_v.at[:, cols], pg_h.at[:, cols])

    backward(0)
    arrive(gl_r, gg_ss.at[0], gg_rs.at[0], sdev)
    chip = gl[c] + gl_r[...]
    gx[...] = jnp.concatenate([chip[:, :256], chip[:, 256:]], axis=0).astype(BF16)
    send(gx, gx_r, gg_ss.at[1], gg_rs.at[1], xdev)
    value = sum_last(0)
    part[0, xo, z] = value.astype(BF16)
    send(part.at[0, xo, z], rxa, rsx_s.at[8], rsx_r.at[8], xdev)
    backward(1)
    arrive(gx_r, gg_ss.at[1], gg_rs.at[1], xdev)
    gz[z] = (gx[...].astype(F32) + gx_r[...].astype(F32)).astype(BF16)
    for k in PEERS:
        send(gz.at[z], gz.at[z], gg_ss.at[1 + k], gg_rs.at[1 + k], dev(xh, zat(k), c))

    counter = jnp.full((1, HALF), step_ref[0, 0] + 1, jnp.int32)

    def power(base):
        total, factor = jnp.ones((1, HALF), F32), jnp.full((1, HALF), base, F32)
        for bit in range(7):
            on = jnp.bitwise_and(jnp.right_shift(counter, bit), 1) == 1
            total = jnp.where(on, total * factor, total)
            factor = factor * factor
        return total

    corr_first, corr_second = 1.0 - power(0.9), 1.0 - power(0.999)

    def update(h, total):
        cols = slice(h * HALF, (h + 1) * HALF)
        first = 0.9 * m1_v[:, cols] + 0.1 * total
        second = 0.999 * m2_v[:, cols] + 0.001 * total * total
        fo_v[:, cols], so_v[:, cols] = first, second
        ratio = first / corr_first / (jnp.sqrt(second / corr_second) + 1e-08)
        master = w_v[:, cols]
        stepped = master - 0.01 * (ratio + 0.1 * master)
        st_v[h] = stepped
        st_s[h] = stepped.astype(BF16)
        send(st_s.at[h], st_r.at[h], go_s.at[h], go_r.at[h], up)
        out(fo_v.at[:, cols], fo_h.at[:, cols])
        out(so_v.at[:, cols], so_h.at[:, cols])

    load_m1.wait()
    load_m2.wait()
    update(1, sum_last(2))
    value = sum_last(1)
    arrive(rxa, rsx_s.at[8], rsx_r.at[8], xdev)
    update(0, value + rxa[...].astype(F32))
    backward(2)
    backward(3)

    for k in PEERS:
        zz = zat(-k)
        arrive(gz.at[zz], gg_ss.at[1 + k], gg_rs.at[1 + k], dev(xh, zz, c))
    total = gz[0].astype(F32)
    for zz in range(1, NZ):
        total += gz[zz].astype(F32)
    gg_o[...] = jnp.concatenate([total[:SEQS], total[SEQS:]], axis=1)
    send(gg_o, gg_r, gg_ss.at[9], gg_rs.at[9], sdev)

    def finish(h):
        cols = slice(h * HALF, (h + 1) * HALF)
        arrive(st_r.at[h], go_s.at[h], go_r.at[h], up)
        wo_v[:, cols] = 0.5 * (st_v[h] + st_r[h].astype(F32))
        out(wo_v.at[:, cols], wo_h.at[:, cols])

    finish(1)
    arrive(gg_r, gg_ss.at[9], gg_rs.at[9], sdev)
    gg_v[c] = gg_o[...]
    gg_v[co] = gg_r[...]
    for h in range(2):
        out(gg_v.at[h], gg_h.at[:, h * HALF:(h + 1) * HALF])
    finish(0)

    for copy in sent:
        copy.wait_send()
    for copy in outs:
        copy.wait()


def fused(shift, place, step, seq_ids, gates, *large):
    vmem, hbm = pltpu.VMEM, pl.ANY
    dma = pltpu.SemaphoreType.DMA
    return pl.pallas_call(
        functools.partial(kernel, shift),
        out_shape=(
            jax.ShapeDtypeStruct((TOK, D), BF16),
            jax.ShapeDtypeStruct((TOK, FFW), BF16),
            jax.ShapeDtypeStruct((SEQS, D), F32),
            jax.ShapeDtypeStruct((ROWS, D), F32),
            jax.ShapeDtypeStruct((ROWS, D), F32),
            jax.ShapeDtypeStruct((ROWS, D), F32),
        ),
        in_specs=[
            pl.BlockSpec(memory_space=pltpu.SMEM),
            pl.BlockSpec(memory_space=vmem),
            pl.BlockSpec(memory_space=vmem),
        ]
        + [pl.BlockSpec(memory_space=hbm)] * 6,
        out_specs=[pl.BlockSpec(memory_space=hbm)] * 6,
        scratch_shapes=[
            vmem((ROWS, D), F32), vmem((ROWS, D), F32), vmem((ROWS, D), F32),
            vmem((TOK, FFW), BF16), vmem((TOK, D), BF16), vmem((TOK, D), BF16),
            vmem((2, 32, ROWS, HALF), BF16),
            vmem((TOK, FFW), BF16), vmem((TOK, FFW), F32),
            vmem((2, NZ, 2, ROWS, TOK), BF16), vmem((2, NZ, ROWS, TOK), BF16),
            vmem((2, TOK, HALF), BF16), vmem((2, TOK, HALF), BF16), vmem((TOK, D), F32),
            vmem((2, 2, NZ, ROWS, HALF), BF16), vmem((24, ROWS, HALF), BF16),
            vmem((NZ, ROWS, HALF), BF16), vmem((ROWS, HALF), BF16),
            vmem((2, SEQS, HALF), F32), vmem((SEQS, HALF), F32),
            vmem((2 * SEQS, HALF // 2), BF16), vmem((2 * SEQS, HALF // 2), BF16),
            vmem((NZ, 2 * SEQS, HALF // 2), BF16), vmem((SEQS, HALF), F32), vmem((SEQS, HALF), F32),
            vmem((2, ROWS, HALF), F32), vmem((2, ROWS, HALF), BF16), vmem((2, ROWS, HALF), BF16),
            vmem((TOK, D), BF16), vmem((TOK, FFW), BF16), vmem((2, SEQS, HALF), F32),
            vmem((ROWS, D), F32), vmem((ROWS, D), F32), vmem((ROWS, D), F32),
            dma((6,)), dma((14,)),
            dma((24,)), dma((24,)), dma((18,)), dma((18,)), dma((36,)), dma((36,)),
            dma((3,)), dma((3,)), dma((24,)), dma((24,)), dma((9,)), dma((9,)),
            dma((10,)), dma((10,)), dma((2,)), dma((2,)),
        ],
        compiler_params=pltpu.CompilerParams(
            collective_id=place, has_side_effects=True, vmem_limit_bytes=48 << 20
        ),
        name="block_step",
    )(step, seq_ids, gates, *large)


def on_device(
    block_input, preact, cotangent, seq_ids, gates, weight, first_moment, second_moment, step
):
    operands = (
        step.reshape(1, 1), seq_ids, gates[0], weight[0], first_moment[0], second_moment[0],
        preact[0], cotangent[0], block_input[0],
    )
    levels = N_GOSSIP.bit_length() - 1
    branches = [functools.partial(fused, 1 << level, level) for level in range(levels)]
    results = lax.switch(lax.rem(step, levels), branches, *operands)
    return tuple(array[None] for array in results)


def solution(mesh):
    split, whole = P("gossip", "fsdp", None), P("gossip", None, None)
    return jax.shard_map(
        on_device,
        mesh=mesh,
        in_specs=(split, split, split, P("gossip", "fsdp"), whole, split, split, split, P()),
        out_specs=(split, split, whole, split, split, split),
        check_vma=False,
    )
```

time: 398 us -> 68.6 us (0.17)
  waiting for transfers between devices: 229 us -> 0 us
  blocking collectives: 124 us -> 0 us
  Pallas kernels: 0 us -> 60.7 us
  matrix products: 15.2 us -> 0 us
  between operations: 14.8 us -> 1.31 us
  other arithmetic: 4.89 us -> 0 us
    reduce_scatter x1 -> x0, waiting for transfers between devices: 135 us -> none  [on_device(): lax.psum_scatter((product * scaling).astype(jnp.bfloat16), 'fsdp', scatte...]
    psum x1 -> x0, blocking collectives: 124 us -> none  [on_device(): lax.psum(gate_local.astype(jnp.bfloat16), 'fsdp').astype(jnp.float32)]
    all_gather x1 -> x0, waiting for transfers between devices: 90.2 us -> none  [on_device(): lax.all_gather(weight_low, 'fsdp', axis=0, tiled=True)]
    pallas_call x0 -> x1, Pallas kernels: none -> 60.7 us  [fused(): pl.pallas_call(functools.partial(kernel, shift), out_shape=(jax.ShapeDtyp...]
    dot_general x5 -> x0, matrix products: 15.2 us -> none  [the longest x1 5.25 us: on_device(): lax.dot_general(scaled_cot, lax.all_gather(weight_low, 'fsdp', axis=0, ti...]
    broadcast_in_dim x4 -> x0, other arithmetic: 4.19 us -> none  [the longest x1 1.89 us: on_device(): second_new[None]]
  transfers between devices with their start and end apart: 3 -> 0, of which waited for: 3 -> 0; matrix products, arithmetic and copies ran while one was open for 1% -> 0% of each run, Pallas kernels for 0% -> 0%
where the time goes in v1:
time: 68.6 us; the launch traced here: 67.3 us
  Pallas kernels  60.7 us (88%)
  local copies, waits for them, and re-layouts  5.02 us (7%)
  between operations  1.31 us (2%)
    pallas_call x1, Pallas kernels, fused(): pl.pallas_call(functools.partial(kernel, shift), out_shape=(jax.ShapeDtyp...  60.7 us
    unnamed x8, local copies, waits for them, and re-layouts  5.02 us

profile of v1, /device:TPU:1, one launch (start us, length us, event | category | flops | bytes accessed | tf_op | source)
XLA Modules:
  0.0 67.3 jit_solution(2163483829700490154)
XLA Ops:
  1.3 0.0 copy-start
  1.3 0.7 copy-done
  2.0 60.9 %conditional.1 = ((bf16[192,1024]{1,0:T(8,128)(2,1)S(1)}, bf16[192,2048]{1,0:T(8,128)(2,1)S(1)}, f32[8,1024]{1,0:T(8,128)S(1)}, f32[64,1024]{1,0:T(8,128)S(1)}, ...) conditional(s32[]{:T(128)} %clamp.3, (s32[1,1]{1,0:T(1,128)}, ...), branch_computations={%region_0.0_spmd, %region_1.0_spmd, %region_2.0_spmd, %region_3.0_... | conditional | bytes 8 | solution.py:445
  2.0 60.7 %block_step.6 = (bf16[192,1024]{1,0:T(8,128)(2,1)S(1)}, bf16[192,2048]{1,0:T(8,128)(2,1)S(1)}, f32[8,1024]{1,0:T(8,128)S(1)}, f32[64,1024]{1,0:T(8,128)S(1)}, f3...) custom-call(s32[1,1]{1,0:T(1,128)} %get-tuple-element.132.step_ref, s32[1,192]{1,0:T(1,128)S(1)} %get-tuple-element.133.seq_ref, ...), custom_call_target="tpu_custom_call" | custom-call | tf_op jit(solution)/shard_map/cond/branch_2_fun/block_step/pallas_call | solution.py:392
  62.9 0.7 %copy.46 = bf16[1,192,1024]{2,1,0:T(8,128)(2,1)} copy(bf16[1,192,1024]{2,1,0:T(8,128)(2,1)S(1)} %bitcast.43) | data formatting | bytes 786432
  63.7 0.9 %copy.47 = bf16[1,192,2048]{2,1,0:T(8,128)(2,1)} copy(bf16[1,192,2048]{2,1,0:T(8,128)(2,1)S(1)} %bitcast.38) | data formatting | bytes 1572864
  64.5 0.6 copy.48
  65.2 0.7 %copy.49 = f32[1,64,1024]{2,1,0:T(8,128)} copy(f32[1,64,1024]{2,1,0:T(8,128)S(1)} %bitcast.44) | data formatting | bytes 524288
  65.9 0.7 %copy.50 = f32[1,64,1024]{2,1,0:T(8,128)} copy(f32[1,64,1024]{2,1,0:T(8,128)S(1)} %bitcast.45) | data formatting | bytes 524288
  66.6 0.7 %copy.51 = f32[1,64,1024]{2,1,0:T(8,128)} copy(f32[1,64,1024]{2,1,0:T(8,128)S(1)} %bitcast.46) | data formatting | bytes 524288
Async XLA Ops:
  1.3 0.7 %copy-start = (s32[1,192]{1,0:T(1,128)S(1)}, s32[1,192]{1,0:T(1,128)}, u32[]{:S(2)}) copy-start(s32[1,192]{1,0:T(1,128)} %param.16) | copy-start | bytes 2308

commit v2 on v0

v2 whole, which is shorter than its diff:
```python
import functools

import jax
import jax.numpy as jnp
from jax import lax
from jax.experimental import pallas as pl
from jax.experimental.pallas import tpu as pltpu
from jax.sharding import PartitionSpec as P

MESH = pl.DeviceIdType.MESH
BF16, F32 = jnp.bfloat16, jnp.float32

TOK, FFW, D, SEQS = 192, 2048, 1024, 8
ROWS, HALF = 64, 512
NZ = 8
N_GOSSIP = 16

GATHER_HOPS = ((4, 3), (3, 4), (4, 3))
SUM_HOPS = ((3, 4), (4, 3), (3, 4))
X_ORDER = (4, 3, -3, 2, -2, 1, -1, 0)
PEERS = tuple(range(1, NZ))
SCHEDULE = (
    ("own", 1, 0), ("own", 1, 1), ("own", 0, 2), ("own", 0, 1), ("gelu", 0), ("own", 0, 0), ("own", 1, 2), ("tg",), ("gelu", 1),
    ("gz", 2, 0, 1), ("gz", 2, 1, 1), ("gx", 0, 0), ("grad", 1, 1), ("xs", 0), ("xs", 1), ("grad", 0, 0), ("gz", 0, 0, 1),
    ("grad", 0, 1), ("grad", 1, 0), ("xs", 2), ("xs", 4), ("rs", 0, 1, 1), ("gz", 0, 1, 1), ("gz", 2, 0, 2), ("own", 0, 3),
    ("gz", 2, 1, 2), ("rs", 1, 0, 1), ("gz", 0, 0, 2), ("rs", 0, 1, 2), ("gz", 1, 0, 1), ("xs", 6), ("gz", 2, 0, 3),
    ("rs", 2, 0, 1), ("rs", 0, 0, 1), ("xs", 3), ("gx", 1, 1), ("rs", 2, 1, 1), ("gx", 1, 0), ("rs", 1, 1, 1), ("gz", 2, 1, 3),
    ("gz", 1, 1, 1), ("gz", 1, 0, 2), ("gz", 0, 1, 2), ("rs", 2, 1, 2), ("gz", 0, 0, 3), ("gz", 2, 0, 4), ("xs", 5),
    ("gx", 1, 2), ("gz", 1, 1, 2), ("gz", 0, 1, 3), ("rs", 0, 1, 3), ("rs", 1, 0, 2), ("gx", 1, 6), ("rs", 0, 0, 2), ("xs", 7),
    ("gx", 1, 3), ("rs", 1, 1, 2), ("gz", 1, 0, 3), ("own", 1, 3), ("rs", 2, 0, 2), ("rs", 2, 1, 3), ("gz", 1, 1, 3),
    ("gx", 1, 7), ("gx", 1, 5), ("gx", 1, 4), ("rs", 0, 1, 4), ("rs", 1, 0, 3), ("rs", 0, 0, 3), ("rs", 2, 1, 4),
    ("rs", 2, 0, 3), ("rs", 1, 1, 3), ("fwd", 1), ("gz", 0, 0, 4), ("gz", 1, 1, 4), ("last", 0), ("rs", 1, 0, 4), ("fwd", 0),
    ("last", 2), ("gate", 0), ("gate", 1), ("last", 1), ("gate", 2), ("bwd", 2), ("gate", 3), ("bwd", 1), ("bwd", 0),
    ("bwd", 3), ("fin", 1), ("gate", 4), ("fin", 0),
)


def kernel(
    shift,
    step_h, seq_h, gates_h, w_h, m1_h, m2_h, pre_h, cot_h, bi_h,
    bo_v, pg_v, gg_v, wo_v, fo_v, so_v,
    step_ref, seq_ref, gates_ref, w_v, m1_v, m2_v, pre_v, cot_v, bi_v,
    wg, hid, slope_v, ht, hts, sc, scs, tg_v,
    part, rz, rx, rxa,
    gl, gl_r, gx, gx_r, gz, gg_o, gg_r,
    st_v, st_s, st_r,
    lsem,
    agz_s, agz_r, agx_s, agx_r, ags_s, ags_r,
    tok_s, tok_r, rsz_s, rsz_r, rsx_s, rsx_r, gg_ss, gg_rs, go_s, go_r,
):
    g = lax.axis_index("gossip")
    f = lax.axis_index("fsdp")
    xh = lax.div(f, 16)
    z = lax.rem(lax.div(f, 2), NZ)
    c = lax.rem(f, 2)
    xo, co = 1 - xh, 1 - c
    scaling = FFW ** -0.5

    def zat(k):
        return lax.rem(z + (k % NZ), NZ)

    def dev(xx, zz, cc):
        return {"fsdp": xx * 16 + zz * 2 + cc}

    znext = (dev(xh, zat(1), c), dev(xh, zat(-1), c))
    xdev, sdev = dev(xo, z, c), dev(xh, z, co)
    up = {"gossip": lax.rem(g + shift, N_GOSSIP)}
    down = {"gossip": lax.rem(g + N_GOSSIP - shift, N_GOSSIP)}

    sent = []

    def describe(src, dst, ssem, rsem, to):
        return pltpu.make_async_remote_copy(
            src_ref=src, dst_ref=dst, send_sem=ssem, recv_sem=rsem, device_id=to, device_id_type=MESH
        )

    def send(src, dst, ssem, rsem, to):
        copy = describe(src, dst, ssem, rsem, to)
        copy.start()
        sent.append(copy)

    def arrive(dst, ssem, rsem, to):
        describe(dst, dst, ssem, rsem, to).wait_recv()

    loads = {}

    def load(name, src, dst):
        loads[name] = pltpu.make_async_copy(src, dst, lsem.at[len(loads)])
        loads[name].start()

    def need(*wanted):
        for name in wanted:
            if name in loads:
                loads.pop(name).wait()
                waited.append(name)

    waited = []
    load("w", w_h, w_v)
    barrier = pltpu.get_barrier_semaphore()
    greeted = [xdev, sdev, down] + [dev(xh, zat(k), c) for k in PEERS]
    for to in greeted:
        pl.semaphore_signal(barrier, inc=1, device_id=to, device_id_type=MESH)
    rest = (
        ("seq", seq_h, seq_ref), ("gates", gates_h, gates_ref), ("cot", cot_h, cot_v), ("pre", pre_h, pre_v),
        ("bi", bi_h, bi_v), ("step", step_h, step_ref), ("m1", m1_h, m1_v), ("m2", m2_h, m2_v),
    )
    for item in rest:
        load(*item)

    def place(h, xx, zz, cc):
        return wg.at[h, xx * 16 + zz * 2 + cc]

    need("w")
    for h in range(2):
        wg[h, f] = w_v[:, h * HALF:(h + 1) * HALF].astype(BF16)
    pl.semaphore_wait(barrier, len(greeted))

    def send_x(h, j, zz):
        block = place(h, xh, zz, c)
        i = 9 * h + j
        send(block, block, agx_s.at[i], agx_r.at[i], xdev)

    def send_s(h, rel, j, xx, zz):
        block = place(h, xx, zz, c)
        i = 18 * h + 9 * rel + j
        send(block, block, ags_s.at[i], ags_r.at[i], sdev)

    def send_z(stream, way, s, h, xx, zz):
        block = place(h, xx, zz, c)
        i = 8 * stream + 4 * way + s - 1
        send(block, block, agz_s.at[i], agz_r.at[i], znext[way])

    def own(h, link):
        if link < 2:
            send_z(2 * h, link, 1, h, xh, z)
        elif link == 2:
            send_x(h, 0, z)
        else:
            send_s(h, 0, 0, xh, z)

    def pass_z(stream, way, s):
        h, xx, rel = ((0, xh, 0), (0, xo, 1), (1, xh, 0))[stream]
        zz = zat(-s if way == 0 else s)
        i = 8 * stream + 4 * way + s - 1
        arrive(place(h, xx, zz, c), agz_s.at[i], agz_r.at[i], znext[way])
        if s < GATHER_HOPS[stream][way]:
            send_z(stream, way, s + 1, h, xx, zz)
        j = 4 * way + s
        if stream == 2:
            send_x(1, j, zz)
        send_s(h, rel, j, xx, zz)

    def offset(j):
        return 0 if j == 0 else -j if j <= 4 else j - 4

    def pass_x(h, j):
        zz = zat(offset(j))
        i = 9 * h + j
        arrive(place(h, xo, zz, c), agx_s.at[i], agx_r.at[i], xdev)
        if h == 0:
            for way in range(2):
                send_z(1, way, 1, 0, xo, zz)
        send_s(h, 1, j, xo, zz)

    def onehot():
        ids = jnp.broadcast_to(seq_ref[...], (SEQS, TOK))
        return jnp.where(lax.broadcasted_iota(jnp.int32, (SEQS, TOK), 0) == ids, 1.0, 0.0).astype(F32)

    def token_gates():
        need("seq", "gates", "cot")
        gates = gates_ref[...]
        hi = gates.astype(BF16).astype(F32)
        mid = (gates - hi).astype(BF16).astype(F32)
        low = (gates - hi - mid).astype(BF16).astype(F32)
        select = jnp.concatenate([onehot()] * 3, axis=0).T.astype(BF16)
        tg_v[...] = jnp.dot(
            select, jnp.concatenate([hi, mid, low], axis=0).astype(BF16), preferred_element_type=F32
        )
        for h in range(2):
            cols = slice(h * HALF, (h + 1) * HALF)
            sc[h] = (tg_v[:, cols] * cot_v[:, cols].astype(F32)).astype(BF16)
        send(sc, scs, tok_s.at[0], tok_r.at[0], sdev)

    def gelu(which):
        need("pre")
        xx = (xo, xh)[which]

        @pl.loop(0, NZ)
        def _(j):
            cols = pl.ds(pl.multiple_of((xx * NZ + j) * 128, 128), 128)
            u = pre_v[:, cols].astype(F32)
            sq = u * u
            th = jnp.tanh(0.7978845608 * (u + 0.044715 * sq * u))
            slope_v[:, cols] = 0.5 * (1.0 + th) + 0.5 * u * (1.0 - th * th) * 0.7978845608 * (
                1.0 + 3.0 * 0.044715 * sq
            )
            low_hidden = (0.5 * u * (1.0 + th)).astype(BF16)
            hid[:, cols] = low_hidden
            ht[xx, j] = low_hidden.T.reshape(2, ROWS, TOK)

        send(ht.at[xx, :, co], hts.at[xx], tok_s.at[1 + which], tok_r.at[1 + which], sdev)

    def once(key, *how):
        if key not in waited:
            waited.append(key)
            arrive(*how)

    def grad(h, rel):
        xx = (xh, xo)[rel]
        k = 2 - rel
        once("scs", scs, tok_s.at[0], tok_r.at[0], sdev)
        once(("hts", rel), hts.at[xx], tok_s.at[k], tok_r.at[k], sdev)
        mine = ht[xx, :, c].reshape(NZ * ROWS, TOK)
        other = hts[xx].reshape(NZ * ROWS, TOK)
        total = jnp.dot(mine, sc[h], preferred_element_type=F32)
        total += jnp.dot(other, scs[h], preferred_element_type=F32)
        part[h, xx] = (total * scaling).astype(BF16).reshape(NZ, ROWS, HALF)

    def sum_x(j):
        send(part.at[1, xo, zat(X_ORDER[j])], rx.at[j], rsx_s.at[j], rsx_r.at[j], xdev)

    sums = ((0, xo), (0, xh), (1, xh))

    def sum_z(stream, way, s):
        h, xx = sums[stream]
        off = (SUM_HOPS[stream][way] - s + 1) * (1 if way == 0 else -1)
        zz = zat(off)
        block = part.at[h, xx, zz]
        i = 8 * stream + 4 * way + s - 1
        if s > 1 or stream == 2:
            value = block[...].astype(F32)
            if stream == 2:
                jx = X_ORDER.index(4 if off == -4 else off)
                arrive(rx.at[jx], rsx_s.at[jx], rsx_r.at[jx], xdev)
                value += rx[jx].astype(F32)
            if s > 1:
                arrive(rz.at[i - 1], rsz_s.at[i - 1], rsz_r.at[i - 1], znext[way])
                value += rz[i - 1].astype(F32)
            block[...] = value.astype(BF16)
        send(block, rz.at[i], rsz_s.at[i], rsz_r.at[i], znext[way])

    def corrections():
        counter = jnp.full((1, HALF), step_ref[0, 0] + 1, jnp.int32)

        def power(base):
            total, factor = jnp.ones((1, HALF), F32), jnp.full((1, HALF), base, F32)
            for bit in range(7):
                on = jnp.bitwise_and(jnp.right_shift(counter, bit), 1) == 1
                total = jnp.where(on, total * factor, total)
                factor = factor * factor
            return total

        return 1.0 - power(0.9), 1.0 - power(0.999)

    def update(h, total):
        need("step", "m1", "m2")
        corr_first, corr_second = corrections()
        cols = slice(h * HALF, (h + 1) * HALF)
        first = 0.9 * m1_v[:, cols] + 0.1 * total
        second = 0.999 * m2_v[:, cols] + 0.001 * total * total
        fo_v[:, cols], so_v[:, cols] = first, second
        ratio = first / corr_first / (jnp.sqrt(second / corr_second) + 1e-08)
        master = w_v[:, cols]
        stepped = master - 0.01 * (ratio + 0.1 * master)
        st_s[h] = stepped.astype(BF16)
        send(st_s.at[h], st_r.at[h], go_s.at[h], go_r.at[h], up)
        st_v[h] = stepped

    def last(stream):
        h, xx = sums[stream]
        value = part[h, xx, z].astype(F32)
        if stream == 2:
            arrive(rx.at[7], rsx_s.at[7], rsx_r.at[7], xdev)
            value += rx[7].astype(F32)
        for way in range(2):
            i = 8 * stream + 4 * way + SUM_HOPS[stream][way] - 1
            arrive(rz.at[i], rsz_s.at[i], rsz_r.at[i], znext[way])
            value += rz[i].astype(F32)
        if stream == 0:
            part[0, xo, z] = value.astype(BF16)
            send(part.at[0, xo, z], rxa, rsx_s.at[8], rsx_r.at[8], xdev)
            return
        if stream == 1:
            arrive(rxa, rsx_s.at[8], rsx_r.at[8], xdev)
            value += rxa[...].astype(F32)
        update(h, value)

    def finish(h):
        cols = slice(h * HALF, (h + 1) * HALF)
        arrive(st_r.at[h], go_s.at[h], go_r.at[h], up)
        wo_v[:, cols] = 0.5 * (st_v[h] + st_r[h].astype(F32))

    def forward(h):
        for rel, xx, stream in ((0, xh, 2 * h), (1, xo, 1 + h)):
            for j in range(9):
                if j == 0 or (j - 1) % 4 < GATHER_HOPS[stream][(j - 1) // 4]:
                    i = 18 * h + 9 * rel + j
                    arrive(place(h, xx, zat(offset(j)), co), ags_s.at[i], ags_r.at[i], sdev)
        need("bi")
        cols = slice(h * HALF, (h + 1) * HALF)
        projected = jnp.dot(hid[...], wg[h].reshape(FFW, HALF), preferred_element_type=F32) * scaling
        bo_v[:, cols] = (bi_v[:, cols].astype(F32) + tg_v[:, cols] * projected).astype(BF16)
        product = cot_v[:, cols].astype(F32) * projected
        hi = product.astype(BF16)
        low = (product - hi.astype(F32)).astype(BF16)
        pick = onehot().astype(BF16)
        gl[h] = jnp.dot(pick, hi, preferred_element_type=F32) + jnp.dot(pick, low, preferred_element_type=F32)

    def gate(stage):
        if stage == 0:
            send(gl.at[co], gl_r, gg_ss.at[0], gg_rs.at[0], sdev)
        elif stage == 1:
            arrive(gl_r, gg_ss.at[0], gg_rs.at[0], sdev)
            chip = gl[c] + gl_r[...]
            gx[...] = jnp.concatenate([chip[:, :256], chip[:, 256:]], axis=0).astype(BF16)
            send(gx, gx_r, gg_ss.at[1], gg_rs.at[1], xdev)
        elif stage == 2:
            arrive(gx_r, gg_ss.at[1], gg_rs.at[1], xdev)
            gz[z] = (gx[...].astype(F32) + gx_r[...].astype(F32)).astype(BF16)
            for k in PEERS:
                send(gz.at[z], gz.at[z], gg_ss.at[1 + k], gg_rs.at[1 + k], dev(xh, zat(k), c))
        elif stage == 3:
            for k in PEERS:
                zz = zat(-k)
                arrive(gz.at[zz], gg_ss.at[1 + k], gg_rs.at[1 + k], dev(xh, zz, c))
            total = gz[0].astype(F32)
            for zz in range(1, NZ):
                total += gz[zz].astype(F32)
            gg_o[...] = jnp.concatenate([total[:SEQS], total[SEQS:]], axis=1)
            send(gg_o, gg_r, gg_ss.at[9], gg_rs.at[9], sdev)
            gg_v[:, pl.ds(pl.multiple_of(c * HALF, HALF), HALF)] = gg_o[...]
        else:
            arrive(gg_r, gg_ss.at[9], gg_rs.at[9], sdev)
            gg_v[:, pl.ds(pl.multiple_of(co * HALF, HALF), HALF)] = gg_r[...]

    def backward(q):
        cols = slice(q * HALF, (q + 1) * HALF)
        total = jnp.zeros((TOK, HALF), F32)
        for h in range(2):
            rows = wg[h, q * 8:(q + 1) * 8].reshape(HALF, HALF)
            total += lax.dot_general(sc[h], rows, (((1,), (1,)), ((), ())), preferred_element_type=F32)
        pg_v[:, cols] = (total * scaling * slope_v[:, cols]).astype(BF16)

    steps = dict(
        own=own, gz=pass_z, gx=pass_x, tg=token_gates, gelu=gelu, grad=grad, xs=sum_x, rs=sum_z,
        last=last, fin=finish, fwd=forward, gate=gate, bwd=backward,
    )
    for name, *detail in SCHEDULE:
        steps[name](*detail)
    for copy in sent:
        copy.wait_send()


def write_kernel(*refs):
    count = len(refs) // 2
    sources, targets, sems = refs[:count], refs[count:2 * count], refs[-1]
    copies = [pltpu.make_async_copy(a, b, sems.at[i]) for i, (a, b) in enumerate(zip(sources, targets))]
    for copy in copies:
        copy.start()
    for copy in copies:
        copy.wait()


def write_out(*arrays):
    return pl.pallas_call(
        write_kernel,
        out_shape=tuple(jax.ShapeDtypeStruct(a.shape, a.dtype) for a in arrays),
        in_specs=[pl.BlockSpec(memory_space=pl.ANY)] * len(arrays),
        out_specs=tuple(pl.BlockSpec(memory_space=pl.ANY) for _ in arrays),
        scratch_shapes=[pltpu.SemaphoreType.DMA((len(arrays),))],
        name="write_out",
    )(*arrays)


def fused(shift, place, *operands):
    vmem = pltpu.VMEM
    dma = pltpu.SemaphoreType.DMA
    return pl.pallas_call(
        functools.partial(kernel, shift),
        out_shape=(
            jax.ShapeDtypeStruct((TOK, D), BF16),
            jax.ShapeDtypeStruct((TOK, FFW), BF16),
            jax.ShapeDtypeStruct((SEQS, D), F32),
            jax.ShapeDtypeStruct((ROWS, D), F32),
            jax.ShapeDtypeStruct((ROWS, D), F32),
            jax.ShapeDtypeStruct((ROWS, D), F32),
        ),
        in_specs=[pl.BlockSpec(memory_space=pltpu.HBM)] * 9,
        out_specs=[pl.BlockSpec(memory_space=vmem)] * 6,
        scratch_shapes=[
            pltpu.SMEM((1, 1), jnp.int32), vmem((1, TOK), jnp.int32), vmem((SEQS, D), F32),
            vmem((ROWS, D), F32), vmem((ROWS, D), F32), vmem((ROWS, D), F32),
            vmem((TOK, FFW), BF16), vmem((TOK, D), BF16), vmem((TOK, D), BF16),
            vmem((2, 32, ROWS, HALF), BF16),
            vmem((TOK, FFW), BF16), vmem((TOK, FFW), F32),
            vmem((2, NZ, 2, ROWS, TOK), BF16), vmem((2, NZ, ROWS, TOK), BF16),
            vmem((2, TOK, HALF), BF16), vmem((2, TOK, HALF), BF16), vmem((TOK, D), F32),
            vmem((2, 2, NZ, ROWS, HALF), BF16), vmem((24, ROWS, HALF), BF16),
            vmem((NZ, ROWS, HALF), BF16), vmem((ROWS, HALF), BF16),
            vmem((2, SEQS, HALF), F32), vmem((SEQS, HALF), F32),
            vmem((2 * SEQS, HALF // 2), BF16), vmem((2 * SEQS, HALF // 2), BF16),
            vmem((NZ, 2 * SEQS, HALF // 2), BF16), vmem((SEQS, HALF), F32), vmem((SEQS, HALF), F32),
            vmem((2, ROWS, HALF), F32), vmem((2, ROWS, HALF), BF16), vmem((2, ROWS, HALF), BF16),
            dma((9,)),
            dma((24,)), dma((24,)), dma((18,)), dma((18,)), dma((36,)), dma((36,)),
            dma((3,)), dma((3,)), dma((24,)), dma((24,)), dma((9,)), dma((9,)),
            dma((10,)), dma((10,)), dma((2,)), dma((2,)),
        ],
        compiler_params=pltpu.CompilerParams(
            collective_id=place, has_side_effects=True, vmem_limit_bytes=48 << 20
        ),
        name="block_step",
    )(*operands)


def on_device(
    block_input, preact, cotangent, seq_ids, gates, weight, first_moment, second_moment, step
):
    operands = (
        step.reshape(1, 1), seq_ids, gates[0], weight[0], first_moment[0], second_moment[0],
        preact[0], cotangent[0], block_input[0],
    )
    levels = N_GOSSIP.bit_length() - 1
    branches = [functools.partial(fused, 1 << level, level) for level in range(levels)]
    results = lax.switch(lax.rem(step, levels), branches, *operands)
    return tuple(array[None] for array in write_out(*results))


def solution(mesh):
    split, whole = P("gossip", "fsdp", None), P("gossip", None, None)
    return jax.shard_map(
        on_device,
        mesh=mesh,
        in_specs=(split, split, split, P("gossip", "fsdp"), whole, split, split, split, P()),
        out_specs=(split, split, whole, split, split, split),
        check_vma=False,
    )
```

time: 398 us -> 64.6 us (0.16); the launches traced: 393 us -> 64.4 us
  waiting for transfers between devices: 229 us -> 0 us
  blocking collectives: 124 us -> 0 us
  Pallas kernels: 0 us -> 62 us
  matrix products: 15.2 us -> 0 us
  between operations: 14.8 us -> 1.49 us
  other arithmetic: 4.89 us -> 0 us
    reduce_scatter x1 -> x0, waiting for transfers between devices: 135 us -> none  [on_device(): lax.psum_scatter((product * scaling).astype(jnp.bfloat16), 'fsdp', scatte...]
    psum x1 -> x0, blocking collectives: 124 us -> none  [on_device(): lax.psum(gate_local.astype(jnp.bfloat16), 'fsdp').astype(jnp.float32)]
    all_gather x1 -> x0, waiting for transfers between devices: 90.2 us -> none  [on_device(): lax.all_gather(weight_low, 'fsdp', axis=0, tiled=True)]
    pallas_call x0 -> x2, Pallas kernels: none -> 62 us  [the longest x1 60.7 us: fused(): pl.pallas_call(functools.partial(kernel, shift), out_shape=(jax.ShapeDtyp...]
    dot_general x5 -> x0, matrix products: 15.2 us -> none  [the longest x1 5.25 us: on_device(): lax.dot_general(scaled_cot, lax.all_gather(weight_low, 'fsdp', axis=0, ti...]
    broadcast_in_dim x4 -> x0, other arithmetic: 4.19 us -> none  [the longest x1 1.89 us: on_device(): second_new[None]]
  transfers between devices with their start and end apart: 3 -> 0, of which waited for: 3 -> 0; matrix products, arithmetic and copies ran while one was open for 1% -> 0% of each run, Pallas kernels for 0% -> 0%
where the time goes in v2:
time: 64.6 us; the launch traced here: 64.4 us
  Pallas kernels  62 us (96%)
  between operations  1.49 us (2%)
  local copies, waits for them, and re-layouts  0.67 us (1%)
    pallas_call x1, Pallas kernels, fused(): pl.pallas_call(functools.partial(kernel, shift), out_shape=(jax.ShapeDtyp...  60.7 us
    pallas_call x1, Pallas kernels, write_out(): pl.pallas_call(write_kernel, out_shape=tuple((jax.ShapeDtypeStruct(a.shap...  1.33 us

profile of v2, /device:TPU:1, one launch (start us, length us, event | category | flops | bytes accessed | tf_op | source)
XLA Modules:
  0.0 64.4 jit_solution(8156727521633728580)
XLA Ops:
  1.3 0.0 copy-start
  1.3 0.7 %copy-done = s32[1,192]{1,0:T(1,128)S(1)} copy-done((s32[1,192]{1,0:T(1,128)S(1)}, s32[1,192]{1,0:T(1,128)}, u32[]{:S(2)}) %copy-start) | copy-done | bytes 792
  2.0 60.9 %conditional.1 = ((bf16[192,1024]{1,0:T(8,128)(2,1)S(1)}, bf16[192,2048]{1,0:T(8,128)(2,1)S(1)}, f32[8,1024]{1,0:T(8,128)S(1)}, f32[64,1024]{1,0:T(8,128)S(1)}, ...) conditional(s32[]{:T(128)} %clamp.3, (s32[1,1]{1,0:T(1,128)}, ...), branch_computations={%region_0.0_spmd, %region_1.0_spmd, %region_2.0_spmd, %region_3.0_... | conditional | bytes 8 | solution.py:425
  2.0 60.7 %block_step.7 = (bf16[192,1024]{1,0:T(8,128)(2,1)S(1)}, bf16[192,2048]{1,0:T(8,128)(2,1)S(1)}, f32[8,1024]{1,0:T(8,128)S(1)}, f32[64,1024]{1,0:T(8,128)S(1)}, f3...) custom-call(s32[1,1]{1,0:T(1,128)} %get-tuple-element.99.step_h, s32[1,192]{1,0:T(1,128)S(1)} %get-tuple-element.100.seq_h, ...), custom_call_target="tpu_custom_call" | custom-call | tf_op jit(solution)/shard_map/cond/branch_3_fun/block_step/pallas_call | solution.py:378
  62.9 1.3 %write_out.1 = (bf16[192,1024]{1,0:T(8,128)(2,1)}, bf16[192,2048]{1,0:T(8,128)(2,1)}, f32[8,1024]{1,0:T(8,128)}, f32[64,1024]{1,0:T(8,128)}, f32[64,1024]{1,0:T(8,128)}, /*index=5*/f32[64,1024]{1,0:T(8,128)}) custom-call(bf16[192,1024]{1,0:T(8,128)(2,1)S(1)} %get-tuple-element.126.refs_0_, bf16[192,2048]{1,0:T(8,128)(2,1)S(1)} %get-tuple-element.127.refs_1_, ...), custom_call_target="tpu_custom_call" | custom-call | tf_op jit(solution)/shard_map/write_out/pallas_call | solution.py:365
Async XLA Ops:
  1.3 0.7 %copy-start = (s32[1,192]{1,0:T(1,128)S(1)}, s32[1,192]{1,0:T(1,128)}, u32[]{:S(2)}) copy-start(s32[1,192]{1,0:T(1,128)} %param.16) | copy-start | bytes 2308

commit v3 on v2

--- a/solution.py
+++ b/solution.py
@@ -20,18 +20,18 @@
 X_ORDER = (4, 3, -3, 2, -2, 1, -1, 0)
 PEERS = tuple(range(1, NZ))
 SCHEDULE = (
-    ("own", 1, 0), ("own", 1, 1), ("own", 0, 2), ("own", 0, 1), ("gelu", 0), ("own", 0, 0), ("own", 1, 2), ("tg",), ("gelu", 1),
-    ("gz", 2, 0, 1), ("gz", 2, 1, 1), ("gx", 0, 0), ("grad", 1, 1), ("xs", 0), ("xs", 1), ("grad", 0, 0), ("gz", 0, 0, 1),
-    ("grad", 0, 1), ("grad", 1, 0), ("xs", 2), ("xs", 4), ("rs", 0, 1, 1), ("gz", 0, 1, 1), ("gz", 2, 0, 2), ("own", 0, 3),
-    ("gz", 2, 1, 2), ("rs", 1, 0, 1), ("gz", 0, 0, 2), ("rs", 0, 1, 2), ("gz", 1, 0, 1), ("xs", 6), ("gz", 2, 0, 3),
-    ("rs", 2, 0, 1), ("rs", 0, 0, 1), ("xs", 3), ("gx", 1, 1), ("rs", 2, 1, 1), ("gx", 1, 0), ("rs", 1, 1, 1), ("gz", 2, 1, 3),
-    ("gz", 1, 1, 1), ("gz", 1, 0, 2), ("gz", 0, 1, 2), ("rs", 2, 1, 2), ("gz", 0, 0, 3), ("gz", 2, 0, 4), ("xs", 5),
-    ("gx", 1, 2), ("gz", 1, 1, 2), ("gz", 0, 1, 3), ("rs", 0, 1, 3), ("rs", 1, 0, 2), ("gx", 1, 6), ("rs", 0, 0, 2), ("xs", 7),
-    ("gx", 1, 3), ("rs", 1, 1, 2), ("gz", 1, 0, 3), ("own", 1, 3), ("rs", 2, 0, 2), ("rs", 2, 1, 3), ("gz", 1, 1, 3),
-    ("gx", 1, 7), ("gx", 1, 5), ("gx", 1, 4), ("rs", 0, 1, 4), ("rs", 1, 0, 3), ("rs", 0, 0, 3), ("rs", 2, 1, 4),
-    ("rs", 2, 0, 3), ("rs", 1, 1, 3), ("fwd", 1), ("gz", 0, 0, 4), ("gz", 1, 1, 4), ("last", 0), ("rs", 1, 0, 4), ("fwd", 0),
-    ("last", 2), ("gate", 0), ("gate", 1), ("last", 1), ("gate", 2), ("bwd", 2), ("gate", 3), ("bwd", 1), ("bwd", 0),
-    ("bwd", 3), ("fin", 1), ("gate", 4), ("fin", 0),
+    ("own", 0, 0), ("own", 0, 2), ("own", 1, 1), ("own", 1, 2), ("gelu", 0), ("own", 1, 0), ("own", 0, 1), ("tg",),
+    ("gz", 0, 0, 1), ("gz", 2, 1, 1), ("grad", 0, 1), ("grad", 1, 1), ("xs", 0), ("gz", 2, 0, 1), ("gx", 0, 0), ("rs", 0, 0, 1),
+    ("rs", 0, 1, 1), ("gz", 2, 1, 2), ("gelu", 1), ("gz", 2, 0, 2), ("xs", 1), ("gz", 1, 1, 1), ("gz", 0, 1, 1), ("grad", 1, 0),
+    ("xs", 2), ("gz", 0, 0, 2), ("xs", 3), ("gz", 1, 0, 1), ("grad", 0, 0), ("rs", 2, 1, 1), ("gx", 1, 2), ("gz", 2, 0, 3),
+    ("rs", 1, 1, 1), ("rs", 1, 0, 1), ("gz", 1, 1, 2), ("gz", 0, 0, 3), ("rs", 0, 1, 2), ("xs", 4), ("gx", 1, 5), ("own", 1, 3),
+    ("gz", 2, 1, 3), ("own", 0, 3), ("gz", 2, 0, 4), ("rs", 2, 1, 2), ("gx", 1, 0), ("gz", 0, 1, 2), ("xs", 5), ("rs", 2, 0, 1),
+    ("gz", 1, 0, 2), ("xs", 6), ("xs", 7), ("gx", 1, 1), ("gx", 1, 3), ("gz", 1, 1, 3), ("rs", 0, 0, 2), ("rs", 0, 1, 3),
+    ("rs", 2, 1, 3), ("gx", 1, 6), ("rs", 1, 0, 2), ("gz", 0, 1, 3), ("gx", 1, 4), ("gx", 1, 7), ("rs", 1, 1, 2),
+    ("rs", 2, 0, 2), ("gz", 0, 0, 4), ("rs", 0, 0, 3), ("gz", 1, 1, 4), ("gz", 1, 0, 3), ("fwd", 1), ("rs", 1, 0, 3),
+    ("rs", 0, 1, 4), ("fwd", 0), ("rs", 2, 1, 4), ("gate", 0), ("rs", 2, 0, 3), ("gate", 1), ("bwd", 3), ("rs", 1, 0, 4),
+    ("rs", 1, 1, 3), ("last", 0), ("last", 2), ("gate", 2), ("bwd", 1), ("bwd", 0), ("bwd", 2), ("last", 1), ("fin", 1),
+    ("gate", 3), ("gate", 4), ("fin", 0),
 )
 
 

time: 64.6 us -> 60.6 us (0.938)
  Pallas kernels: 62 us -> 58 us
    pallas_call x1, Pallas kernels: 60.7 us -> 56.7 us  [fused(): pl.pallas_call(functools.partial(kernel, shift), out_shape=(jax.ShapeDtyp...]
where the time goes in v3:
time: 60.6 us; the launch traced here: 60.4 us
  Pallas kernels  58 us (96%)
  between operations  1.49 us (2%)
  local copies, waits for them, and re-layouts  0.67 us (1%)
    pallas_call x1, Pallas kernels, fused(): pl.pallas_call(functools.partial(kernel, shift), out_shape=(jax.ShapeDtyp...  56.7 us
    pallas_call x1, Pallas kernels, write_out(): pl.pallas_call(write_kernel, out_shape=tuple((jax.ShapeDtypeStruct(a.shap...  1.33 us

profile of v3, /device:TPU:1, one launch (start us, length us, event | category | flops | bytes accessed | tf_op | source)
XLA Modules:
  0.0 60.4 jit_solution(652335660469872905)
XLA Ops:
  1.3 0.0 copy-start
  1.3 0.7 %copy-done = s32[1,192]{1,0:T(1,128)S(1)} copy-done((s32[1,192]{1,0:T(1,128)S(1)}, s32[1,192]{1,0:T(1,128)}, u32[]{:S(2)}) %copy-start) | copy-done | bytes 792
  2.0 56.9 %conditional.1 = ((bf16[192,1024]{1,0:T(8,128)(2,1)S(1)}, bf16[192,2048]{1,0:T(8,128)(2,1)S(1)}, f32[8,1024]{1,0:T(8,128)S(1)}, f32[64,1024]{1,0:T(8,128)S(1)}, ...) conditional(s32[]{:T(128)} %clamp.3, (s32[1,1]{1,0:T(1,128)}, ...), branch_computations={%region_0.0_spmd, %region_1.0_spmd, %region_2.0_spmd, %region_3.0_... | conditional | bytes 8 | solution.py:425
  2.0 56.7 %block_step.6 = (bf16[192,1024]{1,0:T(8,128)(2,1)S(1)}, bf16[192,2048]{1,0:T(8,128)(2,1)S(1)}, f32[8,1024]{1,0:T(8,128)S(1)}, f32[64,1024]{1,0:T(8,128)S(1)}, f3...) custom-call(s32[1,1]{1,0:T(1,128)} %get-tuple-element.90.step_h, s32[1,192]{1,0:T(1,128)S(1)} %get-tuple-element.91.seq_h, ...), custom_call_target="tpu_custom_call" | custom-call | tf_op jit(solution)/shard_map/cond/branch_2_fun/block_step/pallas_call | solution.py:378
  58.9 1.3 %write_out.1 = (bf16[192,1024]{1,0:T(8,128)(2,1)}, bf16[192,2048]{1,0:T(8,128)(2,1)}, f32[8,1024]{1,0:T(8,128)}, f32[64,1024]{1,0:T(8,128)}, f32[64,1024]{1,0:T(8,128)}, /*index=5*/f32[64,1024]{1,0:T(8,128)}) custom-call(bf16[192,1024]{1,0:T(8,128)(2,1)S(1)} %get-tuple-element.126.refs_0_, bf16[192,2048]{1,0:T(8,128)(2,1)S(1)} %get-tuple-element.127.refs_1_, ...), custom_call_target="tpu_custom_call" | custom-call | tf_op jit(solution)/shard_map/write_out/pallas_call | solution.py:365
Async XLA Ops:
  1.3 0.7 %copy-start = (s32[1,192]{1,0:T(1,128)S(1)}, s32[1,192]{1,0:T(1,128)}, u32[]{:S(2)}) copy-start(s32[1,192]{1,0:T(1,128)} %param.16) | copy-start | bytes 2308

commit v4 on v3

--- a/solution.py
+++ b/solution.py
@@ -417,7 +417,7 @@
     block_input, preact, cotangent, seq_ids, gates, weight, first_moment, second_moment, step
 ):
     operands = (
-        step.reshape(1, 1), seq_ids, gates[0], weight[0], first_moment[0], second_moment[0],
+        step.reshape(1, 1), pltpu.with_memory_space_constraint(seq_ids, pltpu.HBM), gates[0], weight[0], first_moment[0], second_moment[0],
         preact[0], cotangent[0], block_input[0],
     )
     levels = N_GOSSIP.bit_length() - 1

time: 60.6 us -> 58.7 us (0.969)
  Pallas kernels: 58 us -> 56.6 us
  local copies, waits for them, and re-layouts: 0.67 us -> 0 us
    pallas_call x1, Pallas kernels: 56.7 us -> 55.2 us  [fused(): pl.pallas_call(functools.partial(kernel, shift), out_shape=(jax.ShapeDtyp...]
    unnamed x2 -> x0, local copies, waits for them, and re-layouts: 0.67 us -> none
where the time goes in v4:
time: 58.7 us; the launch traced here: 58.3 us
  Pallas kernels  56.6 us (96%)
  between operations  1.48 us (3%)
    pallas_call x1, Pallas kernels, fused(): pl.pallas_call(functools.partial(kernel, shift), out_shape=(jax.ShapeDtyp...  55.2 us
    pallas_call x1, Pallas kernels, write_out(): pl.pallas_call(write_kernel, out_shape=tuple((jax.ShapeDtypeStruct(a.shap...  1.33 us

profile of v4, /device:TPU:1, one launch (start us, length us, event | category | flops | bytes accessed | tf_op | source)
XLA Modules:
  0.0 58.3 jit_solution(10648755793085510536)
XLA Ops:
  1.3 55.5 %conditional.1 = ((bf16[192,1024]{1,0:T(8,128)(2,1)S(1)}, bf16[192,2048]{1,0:T(8,128)(2,1)S(1)}, f32[8,1024]{1,0:T(8,128)S(1)}, f32[64,1024]{1,0:T(8,128)S(1)}, ...) conditional(s32[]{:T(128)} %clamp.3, (s32[1,1]{1,0:T(1,128)}, ...), branch_computations={%region_0.0_spmd, %region_1.0_spmd, %region_2.0_spmd, %region_3.0_... | conditional | bytes 8 | solution.py:425
  1.3 55.2 %block_step.5 = (bf16[192,1024]{1,0:T(8,128)(2,1)S(1)}, bf16[192,2048]{1,0:T(8,128)(2,1)S(1)}, f32[8,1024]{1,0:T(8,128)S(1)}, f32[64,1024]{1,0:T(8,128)S(1)}, f3...) custom-call(s32[1,1]{1,0:T(1,128)} %get-tuple-element.81.step_h, s32[1,192]{1,0:T(1,128)} %get-tuple-element.82.seq_h, ...), custom_call_target="tpu_custom_call" | custom-call | tf_op jit(solution)/shard_map/cond/branch_1_fun/block_step/pallas_call | solution.py:378
  56.8 1.3 %write_out.1 = (bf16[192,1024]{1,0:T(8,128)(2,1)}, bf16[192,2048]{1,0:T(8,128)(2,1)}, f32[8,1024]{1,0:T(8,128)}, f32[64,1024]{1,0:T(8,128)}, f32[64,1024]{1,0:T(8,128)}, /*index=5*/f32[64,1024]{1,0:T(8,128)}) custom-call(bf16[192,1024]{1,0:T(8,128)(2,1)S(1)} %get-tuple-element.126.refs_0_, bf16[192,2048]{1,0:T(8,128)(2,1)S(1)} %get-tuple-element.127.refs_1_, ...), custom_call_target="tpu_custom_call" | custom-call | tf_op jit(solution)/shard_map/write_out/pallas_call | solution.py:365

commit v5 on v4

--- a/solution.py
+++ b/solution.py
@@ -20,7 +20,7 @@
 X_ORDER = (4, 3, -3, 2, -2, 1, -1, 0)
 PEERS = tuple(range(1, NZ))
 SCHEDULE = (
-    ("own", 0, 0), ("own", 0, 2), ("own", 1, 1), ("own", 1, 2), ("gelu", 0), ("own", 1, 0), ("own", 0, 1), ("tg",),
+    ("own", 0, 0), ("own", 0, 2), ("own", 1, 1), ("own", 1, 2), ("own", 1, 0), ("own", 0, 1), ("gelu", 0), ("tg",),
     ("gz", 0, 0, 1), ("gz", 2, 1, 1), ("grad", 0, 1), ("grad", 1, 1), ("xs", 0), ("gz", 2, 0, 1), ("gx", 0, 0), ("rs", 0, 0, 1),
     ("rs", 0, 1, 1), ("gz", 2, 1, 2), ("gelu", 1), ("gz", 2, 0, 2), ("xs", 1), ("gz", 1, 1, 1), ("gz", 0, 1, 1), ("grad", 1, 0),
     ("xs", 2), ("gz", 0, 0, 2), ("xs", 3), ("gz", 1, 0, 1), ("grad", 0, 0), ("rs", 2, 1, 1), ("gx", 1, 2), ("gz", 2, 0, 3),
@@ -101,7 +101,7 @@
     for to in greeted:
         pl.semaphore_signal(barrier, inc=1, device_id=to, device_id_type=MESH)
     rest = (
-        ("seq", seq_h, seq_ref), ("gates", gates_h, gates_ref), ("cot", cot_h, cot_v), ("pre", pre_h, pre_v),
+        ("pre", pre_h, pre_v), ("seq", seq_h, seq_ref), ("gates", gates_h, gates_ref), ("cot", cot_h, cot_v),
         ("bi", bi_h, bi_v), ("step", step_h, step_ref), ("m1", m1_h, m1_v), ("m2", m2_h, m2_v),
     )
     for item in rest:

time: 58.7 us -> 59.9 us (1.020); the launches traced: 58.3 us -> 61 us
  Pallas kernels: 56.6 us -> 59.1 us
    pallas_call x1, Pallas kernels: 55.2 us -> 57.8 us  [fused(): pl.pallas_call(functools.partial(kernel, shift), out_shape=(jax.ShapeDtyp...]
where the time goes in v5:
time: 59.9 us; the launch traced here: 61 us
  Pallas kernels  59.1 us (99%)
  between operations  1.48 us (2%)
    pallas_call x1, Pallas kernels, fused(): pl.pallas_call(functools.partial(kernel, shift), out_shape=(jax.ShapeDtyp...  57.8 us
    pallas_call x1, Pallas kernels, write_out(): pl.pallas_call(write_kernel, out_shape=tuple((jax.ShapeDtypeStruct(a.shap...  1.33 us

profile of v5, /device:TPU:1, one launch (start us, length us, event | category | flops | bytes accessed | tf_op | source)
XLA Modules:
  0.0 61.0 jit_solution(10242467814746213614)
XLA Ops:
  1.3 58.2 %conditional.1 = ((bf16[192,1024]{1,0:T(8,128)(2,1)S(1)}, bf16[192,2048]{1,0:T(8,128)(2,1)S(1)}, f32[8,1024]{1,0:T(8,128)S(1)}, f32[64,1024]{1,0:T(8,128)S(1)}, ...) conditional(s32[]{:T(128)} %clamp.3, (s32[1,1]{1,0:T(1,128)}, ...), branch_computations={%region_0.0_spmd, %region_1.0_spmd, %region_2.0_spmd, %region_3.0_... | conditional | bytes 8 | solution.py:425
  1.5 57.8 %block_step.7 = (bf16[192,1024]{1,0:T(8,128)(2,1)S(1)}, bf16[192,2048]{1,0:T(8,128)(2,1)S(1)}, f32[8,1024]{1,0:T(8,128)S(1)}, f32[64,1024]{1,0:T(8,128)S(1)}, f3...) custom-call(s32[1,1]{1,0:T(1,128)} %get-tuple-element.99.step_h, s32[1,192]{1,0:T(1,128)} %get-tuple-element.100.seq_h, ...), custom_call_target="tpu_custom_call" | custom-call | tf_op jit(solution)/shard_map/cond/branch_3_fun/block_step/pallas_call | solution.py:378
  59.5 1.3 %write_out.1 = (bf16[192,1024]{1,0:T(8,128)(2,1)}, bf16[192,2048]{1,0:T(8,128)(2,1)}, f32[8,1024]{1,0:T(8,128)}, f32[64,1024]{1,0:T(8,128)}, f32[64,1024]{1,0:T(8,128)}, /*index=5*/f32[64,1024]{1,0:T(8,128)}) custom-call(bf16[192,1024]{1,0:T(8,128)(2,1)S(1)} %get-tuple-element.126.refs_0_, bf16[192,2048]{1,0:T(8,128)(2,1)S(1)} %get-tuple-element.127.refs_1_, ...), custom_call_target="tpu_custom_call" | custom-call | tf_op jit(solution)/shard_map/write_out/pallas_call | solution.py:365
